TPU v7x, 32 devices: a whole 2x2x4 slice. The times are simulated.
32 devices in a mesh: dp: 16 (over z, x, core), tensor: 2 (over y).
Axes of the slice: x: 2, y: 2, z: 4, core: 2. Of those that a mesh axis runs over, the one named last changes fastest.
Arguments:
- clean_images: bfloat16 [64, 256, 768], P(('dp', 'tensor')), may hold values from -6 to 6
- noise_draw: bfloat16 [64, 256, 768], P(('dp', 'tensor')), may hold values from -6 to 6
- levels: int32 [64], P(('dp', 'tensor')), may hold values from 0 to 999
- labels: int32 [64], P(('dp', 'tensor')), may hold values from 0 to 999
- dropped: int32 [64], P(('dp', 'tensor')), may hold values 0 or 1
- groups: int32 [64], P(('dp', 'tensor')), may hold values from 0 to 3
- step_count: int32 [1], replicated, may hold values from 1 to 20
- inward: float32 [1024, 3, 1024], P('dp', None, 'tensor'), may hold values from -0.1875 to 0.1875
- first_inward: float32 [1024, 3, 1024], P('dp', None, 'tensor'), may hold values from -2.744419e-06 to 2.744419e-06, as said below
- second_inward: float32 [1024, 3, 1024], P('dp', None, 'tensor'), may hold values from 3.347482e-12 to 1.3389928e-11
- outward: float32 [1024, 1024], P('tensor', 'dp'), may hold values from -0.75 to 0.75
- first_outward: float32 [1024, 1024], P('tensor', 'dp'), may hold values from -1.3722094e-06 to 1.3722094e-06, as said below
- second_outward: float32 [1024, 1024], P('tensor', 'dp'), may hold values from 8.368705e-13 to 3.347482e-12
- expand: float32 [1024, 2, 3072], P('dp', None, 'tensor'), may hold values from -0.1875 to 0.1875
- first_expand: float32 [1024, 2, 3072], P('dp', None, 'tensor'), may hold values from -1.029157e-06 to 1.029157e-06, as said below
- second_expand: float32 [1024, 2, 3072], P('dp', None, 'tensor'), may hold values from 4.7073966e-13 to 1.8829586e-12
- shrink: float32 [3072, 1024], P('tensor', 'dp'), may hold values from -0.109375 to 0.109375
- first_shrink: float32 [3072, 1024], P('tensor', 'dp'), may hold values from -2.744419e-06 to 2.744419e-06, as said below
- second_shrink: float32 [3072, 1024], P('tensor', 'dp'), may hold values from 3.347482e-12 to 1.3389928e-11
- patches: float32 [2, 768, 1024], P(None, ('dp', 'tensor')), may hold values from -0.1875 to 0.1875
- first_patches: float32 [2, 768, 1024], P(None, ('dp', 'tensor')), may hold values from -6.861047e-06 to 6.861047e-06, as said below
- second_patches: float32 [2, 768, 1024], P(None, ('dp', 'tensor')), may hold values from 2.0921763e-11 to 8.368705e-11
- classes: float32 [1001, 768], P(None, ('dp', 'tensor')), may hold values from -0.21875 to 0.21875
- first_classes: float32 [1001, 768], P(None, ('dp', 'tensor')), may hold values from -6.861047e-06 to 6.861047e-06, as said below
- second_classes: float32 [1001, 768], P(None, ('dp', 'tensor')), may hold values from 2.0921763e-11 to 8.368705e-11
- mapping: float32 [768, 4096], P(('dp', 'tensor')), may hold values from -0.21875 to 0.21875
- first_mapping: float32 [768, 4096], P(('dp', 'tensor')), may hold values from -6.861047e-06 to 6.861047e-06, as said below
- second_mapping: float32 [768, 4096], P(('dp', 'tensor')), may hold values from 2.0921763e-11 to 8.368705e-11
Outputs:
- total_loss: float32 [], replicated
- grad_norm: float32 [], replicated
- inward_next: float32 [1024, 3, 1024], P('dp', None, 'tensor')
- moment_inward: float32 [1024, 3, 1024], P('dp', None, 'tensor')
- square_inward: float32 [1024, 3, 1024], P('dp', None, 'tensor')
- outward_next: float32 [1024, 1024], P('tensor', 'dp')
- moment_outward: float32 [1024, 1024], P('tensor', 'dp')
- square_outward: float32 [1024, 1024], P('tensor', 'dp')
- expand_next: float32 [1024, 2, 3072], P('dp', None, 'tensor')
- moment_expand: float32 [1024, 2, 3072], P('dp', None, 'tensor')
- square_expand: float32 [1024, 2, 3072], P('dp', None, 'tensor')
- shrink_next: float32 [3072, 1024], P('tensor', 'dp')
- moment_shrink: float32 [3072, 1024], P('tensor', 'dp')
- square_shrink: float32 [3072, 1024], P('tensor', 'dp')
- patches_next: float32 [2, 768, 1024], P(None, ('dp', 'tensor'))
- moment_patches: float32 [2, 768, 1024], P(None, ('dp', 'tensor'))
- square_patches: float32 [2, 768, 1024], P(None, ('dp', 'tensor'))
- classes_next: float32 [1001, 768], P(None, ('dp', 'tensor'))
- moment_classes: float32 [1001, 768], P(None, ('dp', 'tensor'))
- square_classes: float32 [1001, 768], P(None, ('dp', 'tensor'))
- mapping_next: float32 [768, 4096], P(('dp', 'tensor'))
- moment_mapping: float32 [768, 4096], P(('dp', 'tensor'))
- square_mapping: float32 [768, 4096], P(('dp', 'tensor'))
Inputs may be any that keep to these rules, and one draw needn't show every extreme that they name: `first_inward`: entries of both signs. `first_outward`: entries of both signs. `first_expand`: entries of both signs. `first_shrink`: entries of both signs. `first_patches`: entries of both signs. `first_classes`: entries of both signs. `first_mapping`: entries of both signs.
All inputs are finite; a program needn't handle non-finite values. No bound on the sum of `dropped` on one device may be relied on, other than what follows from the above.
Results may differ from a plain program's by a relative error of at most 0.012.
Values may be sent and summed in bfloat16 or wider, within the bound.
No kernel may reach another device: no remote copies, remote signals or barrier semaphores. Data moves between devices by JAX's collectives and lax.ppermute only.
A program may use at most 256 MiB of HBM per device.

v0:
```python
import math
import jax
import jax.numpy as jnp
from jax import lax
from jax.sharding import PartitionSpec as P

D = 1024
HEAD_DIM = 64
CD = 768
CLASSES = 1001
PD = 768
FOUR = 256
SEQ = 256
GROUPS = 4
NLEVELS = 1000
HIGH = lax.Precision.HIGHEST
SIGMA_DATA = 0.5
LEARN_RATE = 0.05
DECAY = 0.1
BETA_ONE = 0.5
BETA_TWO = 0.5
ADAM_EPS = 1e-08
CLIP = 0.02
NORM_EPS = 1e-06


def to_low(value):
    return value.astype(jnp.bfloat16).astype(jnp.float32)


def rms_norm(value):
    return value * lax.rsqrt(jnp.mean(value * value, axis=-1, keepdims=True) + NORM_EPS)


def einsum_low(form, left, right):
    return jnp.einsum(form, left, right, preferred_element_type=jnp.float32)


def outer_sum(left, right):
    return jnp.dot(left.T, right, precision=HIGH)


def noise_terms(levels):
    log_sigma = -3.0 + 6.0 * levels.astype(jnp.float32) / (NLEVELS - 1)
    sigma = jnp.exp(log_sigma)
    radius = jnp.sqrt(sigma * sigma + SIGMA_DATA * SIGMA_DATA)
    half = FOUR // 2
    freqs = jnp.exp(-2.0 + 4.0 * jnp.arange(half, dtype=jnp.float32) / (half - 1))
    angles = 2.0 * math.pi * (log_sigma / 4.0)[:, None] * freqs[None, :]
    return (sigma, radius, jnp.concatenate([jnp.cos(angles), jnp.sin(angles)], axis=1))


def map_forward(feats, onehot, table, mats):
    feats_low = to_low(feats)
    cond_zero = jnp.dot(onehot, table, precision=HIGH) + jnp.dot(
        feats_low, mats[:, :FOUR].T, precision=HIGH
    )
    normed = to_low(rms_norm(cond_zero))
    inner = jnp.dot(normed, mats[:, FOUR : FOUR + CD], precision=HIGH)
    cond_low = to_low(cond_zero + jax.nn.gelu(inner))
    scales = 1.0 + jnp.dot(cond_low, mats[:, FOUR + CD :], precision=HIGH)
    return (scales, (feats_low, cond_zero, normed, inner, cond_low))


def map_backward(mats, kept, grad_scales):
    feats_low, cond_zero, normed, inner, cond_low = kept
    grad_cond = jnp.dot(grad_scales, mats[:, FOUR + CD :].T, precision=HIGH)
    _, pull_gelu = jax.vjp(jax.nn.gelu, inner)
    (grad_inner,) = pull_gelu(grad_cond)
    grad_normed = jnp.dot(grad_inner, mats[:, FOUR : FOUR + CD].T, precision=HIGH)
    _, pull_norm = jax.vjp(rms_norm, cond_zero)
    (grad_zero,) = pull_norm(grad_normed)
    return (grad_zero + grad_cond, grad_inner)


def scale_norm(hidden, scale):
    return rms_norm(hidden) * scale[:, None, :]


def norm_back(hidden, scale, grad):
    _, pull = jax.vjp(scale_norm, hidden, scale)
    return pull(grad)


def pair_rows(value):
    return lax.all_gather(value, "tensor", axis=0, tiled=True)


def pair_sum(value):
    return lax.psum_scatter(value, "tensor", scatter_dimension=0, tiled=True)


def split_heads(project):
    images, tokens = (project.shape[0], project.shape[1])
    heads = project.shape[3] // HEAD_DIM
    return tuple(
        (project[:, :, part].reshape(images, tokens, heads, HEAD_DIM) for part in range(3))
    )


def attention_probs(queries, keys, totals):
    scores = einsum_low("iqhe,ikhe->ihqk", queries, keys) * (1.0 / math.sqrt(HEAD_DIM))
    return jnp.exp(scores - totals)


def layer_forward(big, patch_pair, inputs, scales):
    attn_in, attn_out, gate_up, down = big
    resid_zero = einsum_low("isp,pd->isd", inputs, patch_pair[0])
    rows_zero = pair_rows(scale_norm(resid_zero, scales[:, 0]).astype(jnp.bfloat16))
    project = einsum_low("isd,dke->iske", rows_zero, attn_in).astype(jnp.bfloat16)
    queries, keys, values = split_heads(project)
    scores = einsum_low("iqhe,ikhe->ihqk", queries, keys) * (1.0 / math.sqrt(HEAD_DIM))
    totals = jax.nn.logsumexp(scores, axis=-1, keepdims=True)
    probs = jnp.exp(scores - totals).astype(jnp.bfloat16)
    mixed = einsum_low("ihqk,ikhe->iqhe", probs, values).astype(jnp.bfloat16)
    mixed = mixed.reshape(mixed.shape[0], mixed.shape[1], -1)
    resid_one = resid_zero + pair_sum(einsum_low("isd,de->ise", mixed, attn_out))
    rows_one = pair_rows(scale_norm(resid_one, scales[:, 1]).astype(jnp.bfloat16))
    gated = einsum_low("isd,dkf->iskf", rows_one, gate_up)
    hidden = (jax.nn.gelu(gated[:, :, 0]) * gated[:, :, 1]).astype(jnp.bfloat16)
    resid_two = resid_one + pair_sum(einsum_low("isf,fd->isd", hidden, down))
    last = scale_norm(resid_two, scales[:, 2]).astype(jnp.bfloat16)
    output = einsum_low("isd,pd->isp", last, patch_pair[1])
    return (
        resid_zero,
        rows_zero,
        project,
        totals,
        mixed,
        resid_one,
        rows_one,
        gated,
        hidden,
        resid_two,
        last,
        output,
    )


def layer_backward(big, patch_pair, inputs, scales, kept, grad_out):
    attn_in, attn_out, gate_up, down = big
    (
        resid_zero,
        rows_zero,
        project,
        totals,
        mixed,
        resid_one,
        rows_one,
        gated,
        hidden,
        resid_two,
        last,
        output,
    ) = kept
    grad_low = grad_out.astype(jnp.bfloat16)
    grad_last = einsum_low("isp,pd->isd", grad_low, patch_pair[1])
    grad_patch_out = einsum_low("isp,isd->pd", grad_low, last)
    grad_two, scale_two = norm_back(resid_two, scales[:, 2], grad_last)
    rows_grad = pair_rows(grad_two.astype(jnp.bfloat16))
    grad_hidden = einsum_low("isd,fd->isf", rows_grad, down)
    grad_down = einsum_low("isf,isd->fd", hidden, rows_grad)
    _, pull_gate = jax.vjp(
        lambda gate, upper: jax.nn.gelu(gate) * upper, gated[:, :, 0], gated[:, :, 1]
    )
    grad_gate, grad_up = pull_gate(grad_hidden)
    grad_gated = jnp.stack([grad_gate, grad_up], axis=2).astype(jnp.bfloat16)
    grad_gate_up = einsum_low("isd,iskf->dkf", rows_one, grad_gated)
    part_one, scale_one = norm_back(
        resid_one, scales[:, 1], pair_sum(einsum_low("iskf,dkf->isd", grad_gated, gate_up))
    )
    grad_one = grad_two + part_one
    rows_grad = pair_rows(grad_one.astype(jnp.bfloat16))
    queries, keys, values = split_heads(project)
    grad_mixed = (
        einsum_low("isd,ed->ise", rows_grad, attn_out).astype(jnp.bfloat16).reshape(queries.shape)
    )
    grad_attn_out = einsum_low("ise,isd->ed", mixed, rows_grad)
    probs = attention_probs(queries, keys, totals)
    grad_values = einsum_low("ihqk,iqhe->ikhe", probs.astype(jnp.bfloat16), grad_mixed)
    grad_probs = einsum_low("iqhe,ikhe->ihqk", grad_mixed, values)
    grad_scores = (
        probs * (grad_probs - jnp.sum(grad_probs * probs, axis=-1, keepdims=True))
    ).astype(jnp.bfloat16)
    inverse_root = 1.0 / math.sqrt(HEAD_DIM)
    grad_queries = einsum_low("ihqk,ikhe->iqhe", grad_scores, keys) * inverse_root
    grad_keys = einsum_low("ihqk,iqhe->ikhe", grad_scores, queries) * inverse_root
    grad_project = jnp.stack([grad_queries, grad_keys, grad_values], axis=2)
    grad_project = grad_project.reshape(project.shape).astype(jnp.bfloat16)
    grad_attn_in = einsum_low("isd,iske->dke", rows_zero, grad_project)
    part_zero, scale_zero = norm_back(
        resid_zero, scales[:, 0], pair_sum(einsum_low("iske,dke->isd", grad_project, attn_in))
    )
    grad_zero = (grad_one + part_zero).astype(jnp.bfloat16)
    grad_patch_in = einsum_low("isp,isd->pd", inputs, grad_zero)
    grad_scales = jnp.stack([scale_zero, scale_one, scale_two], axis=1)
    return (
        (grad_attn_in, grad_attn_out, grad_gate_up, grad_down),
        jnp.stack([grad_patch_in, grad_patch_out]),
        grad_scales,
    )


def body(
    clean_images,
    noise_draw,
    levels,
    labels,
    dropped,
    groups,
    step_count,
    inward,
    first_inward,
    second_inward,
    outward,
    first_outward,
    second_outward,
    expand,
    first_expand,
    second_expand,
    shrink,
    first_shrink,
    second_shrink,
    patches,
    first_patches,
    second_patches,
    classes,
    first_classes,
    second_classes,
    mapping,
    first_mapping,
    second_mapping,
):
    masters = (inward, outward, expand, shrink, patches, classes, mapping)
    firsts = (
        first_inward,
        first_outward,
        first_expand,
        first_shrink,
        first_patches,
        first_classes,
        first_mapping,
    )
    seconds = (
        second_inward,
        second_outward,
        second_expand,
        second_shrink,
        second_patches,
        second_classes,
        second_mapping,
    )
    big = (
        lax.all_gather(inward.astype(jnp.bfloat16), "dp", axis=0, tiled=True),
        lax.all_gather(outward.astype(jnp.bfloat16), "dp", axis=1, tiled=True),
        lax.all_gather(expand.astype(jnp.bfloat16), "dp", axis=0, tiled=True),
        lax.all_gather(shrink.astype(jnp.bfloat16), "dp", axis=1, tiled=True),
    )
    small = (
        lax.all_gather(patches.astype(jnp.bfloat16), ("dp", "tensor"), axis=1, tiled=True),
        lax.all_gather(classes.astype(jnp.bfloat16), ("dp", "tensor"), axis=1, tiled=True),
        lax.all_gather(mapping.astype(jnp.bfloat16), ("dp", "tensor"), axis=0, tiled=True),
    )
    sigma, radius, feats = noise_terms(levels)
    chosen = jnp.where(dropped == 1, CLASSES - 1, labels)
    onehot = (chosen[:, None] == jnp.arange(CLASSES)[None, :]).astype(jnp.float32)
    map_mats = small[2].astype(jnp.float32)
    scale_flat, map_kept = map_forward(feats, onehot, small[1].astype(jnp.float32), map_mats)
    scales = scale_flat.reshape(-1, 3, D)
    sig = sigma[:, None, None]
    rad = radius[:, None, None]
    clean_float = clean_images.astype(jnp.float32)
    noise_float = noise_draw.astype(jnp.float32)
    inputs = ((clean_float + sig * noise_float) / rad).astype(jnp.bfloat16)
    target = (sig * clean_float - SIGMA_DATA * SIGMA_DATA * noise_float) / (SIGMA_DATA * rad)
    kept = layer_forward(big, small[0], inputs, scales)
    output = kept[-1]
    counts = jnp.sum((groups[:, None] == groups[None, :]).astype(jnp.float32), axis=1)
    weight = 1.0 / (GROUPS * counts)
    local_loss = jnp.sum(weight * jnp.mean((output - target) ** 2, axis=(1, 2)))
    total_loss = lax.psum(local_loss, ("dp", "tensor"))
    grad_out = 2.0 * (output - target) * (weight / (SEQ * PD))[:, None, None]
    backward_big = (
        lax.all_gather(inward.astype(jnp.bfloat16), "dp", axis=0, tiled=True),
        lax.all_gather(outward.astype(jnp.bfloat16), "dp", axis=1, tiled=True),
        lax.all_gather(expand.astype(jnp.bfloat16), "dp", axis=0, tiled=True),
        lax.all_gather(shrink.astype(jnp.bfloat16), "dp", axis=1, tiled=True),
    )
    big_grads, patch_grads, scale_grads = layer_backward(
        backward_big, small[0], inputs, scales, kept, grad_out
    )
    grad_scales = scale_grads.reshape(-1, 3 * D)
    grad_zero, grad_inner = map_backward(map_mats, map_kept, grad_scales)
    feats_low, cond_zero, normed, inner, cond_low = map_kept
    big_shards = (
        lax.psum_scatter(big_grads[0], "dp", scatter_dimension=0, tiled=True),
        lax.psum_scatter(big_grads[1], "dp", scatter_dimension=1, tiled=True),
        lax.psum_scatter(big_grads[2], "dp", scatter_dimension=0, tiled=True),
        lax.psum_scatter(big_grads[3], "dp", scatter_dimension=1, tiled=True),
    )
    table_grad = outer_sum(onehot, grad_zero)
    mapping_grad = jnp.concatenate(
        [
            outer_sum(grad_zero, feats_low),
            outer_sum(normed, grad_inner),
            outer_sum(cond_low, grad_scales),
        ],
        axis=1,
    )
    small_shards = (
        lax.psum_scatter(patch_grads, ("dp", "tensor"), scatter_dimension=1, tiled=True),
        lax.psum_scatter(table_grad, ("dp", "tensor"), scatter_dimension=1, tiled=True),
        lax.psum_scatter(mapping_grad, ("dp", "tensor"), scatter_dimension=0, tiled=True),
    )
    grads = tuple(big_shards) + tuple(small_shards)
    squares = sum((jnp.sum(grad * grad) for grad in grads))
    squares_total = lax.psum(squares, ("dp", "tensor"))
    grad_norm = jnp.sqrt(squares_total)
    factor = CLIP / (grad_norm + NORM_EPS)
    count = step_count[0].astype(jnp.float32)
    fix_one = 1.0 - jnp.power(BETA_ONE, count)
    fix_two = 1.0 - jnp.power(BETA_TWO, count)
    results = [total_loss, grad_norm]
    for master, first, second, grad in zip(masters, firsts, seconds, grads):
        clipped = grad * factor
        moment = BETA_ONE * first + (1.0 - BETA_ONE) * clipped
        square = BETA_TWO * second + (1.0 - BETA_TWO) * clipped * clipped
        step_size = moment / fix_one / (jnp.sqrt(square / fix_two) + ADAM_EPS)
        results.extend([master - LEARN_RATE * (step_size + DECAY * master), moment, square])
    return tuple(results)


def solution(mesh):
    in_specs = (
        P(("dp", "tensor"), None, None),
        P(("dp", "tensor"), None, None),
        P(("dp", "tensor")),
        P(("dp", "tensor")),
        P(("dp", "tensor")),
        P(("dp", "tensor")),
        P(),
        P("dp", None, "tensor"),
        P("dp", None, "tensor"),
        P("dp", None, "tensor"),
        P("tensor", "dp"),
        P("tensor", "dp"),
        P("tensor", "dp"),
        P("dp", None, "tensor"),
        P("dp", None, "tensor"),
        P("dp", None, "tensor"),
        P("tensor", "dp"),
        P("tensor", "dp"),
        P("tensor", "dp"),
        P(None, ("dp", "tensor"), None),
        P(None, ("dp", "tensor"), None),
        P(None, ("dp", "tensor"), None),
        P(None, ("dp", "tensor")),
        P(None, ("dp", "tensor")),
        P(None, ("dp", "tensor")),
        P(("dp", "tensor"), None),
        P(("dp", "tensor"), None),
        P(("dp", "tensor"), None),
    )
    out_specs = (
        P(),
        P(),
        P("dp", None, "tensor"),
        P("dp", None, "tensor"),
        P("dp", None, "tensor"),
        P("tensor", "dp"),
        P("tensor", "dp"),
        P("tensor", "dp"),
        P("dp", None, "tensor"),
        P("dp", None, "tensor"),
        P("dp", None, "tensor"),
        P("tensor", "dp"),
        P("tensor", "dp"),
        P("tensor", "dp"),
        P(None, ("dp", "tensor"), None),
        P(None, ("dp", "tensor"), None),
        P(None, ("dp", "tensor"), None),
        P(None, ("dp", "tensor")),
        P(None, ("dp", "tensor")),
        P(None, ("dp", "tensor")),
        P(("dp", "tensor"), None),
        P(("dp", "tensor"), None),
        P(("dp", "tensor"), None),
    )
    return jax.shard_map(body, mesh=mesh, in_specs=in_specs, out_specs=out_specs, check_vma=False)
```

profile of v0, /device:TPU:0, one launch (start us, length us, event | category | flops | bytes accessed | tf_op | source)
XLA Modules:
  0.0 1666.4 jit_solution(6635196143196874810)
XLA Ops:
  16.0 57.3 %all-gather.12.cloned.1.call-done = bf16[2,768,1024]{2,1,0:T(8,128)(2,1)} async-done(((bf16[2,24,1024]{2,1,0:T(8,128)(2,1)}), bf16[2,768,1024]{2,1,0:T(8,128)(2,1)}) %all-gather.12.cloned.1.call-update) | async-done | bytes 3145744 | tf_op jit(solution)/shard_map/all_gather | solution.py:260
  76.4 68.7 %all-gather.16.cloned.1.call-done = bf16[768,4096]{1,0:T(8,128)(2,1)} async-done(((bf16[24,4096]{1,0:T(8,128)(2,1)}), bf16[768,4096]{1,0:T(8,128)(2,1)}) %all-gather.16.cloned.1.call-update) | async-done | bytes 6291472 | tf_op jit(solution)/shard_map/all_gather | solution.py:262
  146.3 55.9 %all-gather.14.cloned.1.call-done = bf16[1001,768]{0,1:T(8,128)(2,1)} async-done(((bf16[1001,24]{0,1:T(8,128)(2,1)}), bf16[1001,768]{0,1:T(8,128)(2,1)}) %all-gather.14.cloned.1.call-update) | async-done | bytes 1537552 | tf_op jit(solution)/shard_map/all_gather | solution.py:261
  212.2 36.7 %all-gather.20.cloned.1.call-done = bf16[1024,3,512]{2,0,1:T(8,128)(2,1)} async-done(((bf16[64,3,512]{2,0,1:T(8,128)(2,1)}), bf16[1024,3,512]{2,0,1:T(8,128)(2,1)}) %all-gather.20.cloned.1.call-update) | async-done | bytes 3145744 | tf_op jit(solution)/shard_map/all_gather | solution.py:254
  248.9 33.4 %all-gather.18.cloned.1.call-done = bf16[4,256,1024]{2,1,0:T(8,128)(2,1)} async-done(((bf16[2,256,1024]{2,1,0:T(8,128)(2,1)}), bf16[4,256,1024]{2,1,0:T(8,128)(2,1)}) %all-gather.18.cloned.1.call-update) | async-done | bytes 2097168 | tf_op jit(solution)/shard_map/all_gather | solution.py:86
  298.6 24.3 %all-gather.22.cloned.1.call-done = bf16[512,1024]{0,1:T(8,128)(2,1)} async-done(((bf16[512,64]{0,1:T(8,128)(2,1)}), bf16[512,1024]{0,1:T(8,128)(2,1)}) %all-gather.22.cloned.1.call-update) | async-done | bytes 1048592 | tf_op jit(solution)/shard_map/all_gather | solution.py:255
  329.9 50.9 %reduce-scatter.12.cloned.1.call-done = f32[2,256,1024]{2,1,0:T(8,128)} async-done(((f32[4,256,1024]{2,1,0:T(8,128)}), f32[2,256,1024]{2,1,0:T(8,128)}) %reduce-scatter.12.cloned.1.call-update) | async-done | bytes 2097168 | tf_op jit(solution)/shard_map/reduce_scatter | solution.py:90
  386.5 59.3 %all-gather.26.cloned.1.call-done = bf16[1024,2,1536]{2,0,1:T(8,128)(2,1)} async-done(((bf16[64,2,1536]{2,0,1:T(8,128)(2,1)}), bf16[1024,2,1536]{2,0,1:T(8,128)(2,1)}) %all-gather.26.cloned.1.call-update) | async-done | bytes 6291472 | tf_op jit(solution)/shard_map/all_gather | solution.py:256
  445.9 33.4 %all-gather.24.cloned.1.call-done = bf16[4,256,1024]{2,1,0:T(8,128)(2,1)} async-done(((bf16[2,256,1024]{2,1,0:T(8,128)(2,1)}), bf16[4,256,1024]{2,1,0:T(8,128)(2,1)}) %all-gather.24.cloned.1.call-update) | async-done | bytes 2097168 | tf_op jit(solution)/shard_map/all_gather | solution.py:86
  479.2 9.4 fusion.9
  496.6 31.1 %all-gather.28.cloned.1.call-done = bf16[1536,1024]{0,1:T(8,128)(2,1)} async-done(((bf16[1536,64]{0,1:T(8,128)(2,1)}), bf16[1536,1024]{0,1:T(8,128)(2,1)}) %all-gather.28.cloned.1.call-update) | async-done | bytes 3145744 | tf_op jit(solution)/shard_map/all_gather | solution.py:257
  527.6 8.4 fusion.24
  536.9 52.4 %reduce-scatter.14.cloned.1.call-done = f32[2,256,1024]{2,1,0:T(8,128)} async-done(((f32[4,256,1024]{2,1,0:T(8,128)}), f32[2,256,1024]{2,1,0:T(8,128)}) %reduce-scatter.14.cloned.1.call-update) | async-done | bytes 2097168 | tf_op jit(solution)/shard_map/reduce_scatter | solution.py:90
  597.9 33.2 %all-gather.30.cloned.1.call-done = bf16[4,256,1024]{2,1,0:T(8,128)(2,1)} async-done(((bf16[2,256,1024]{2,1,0:T(8,128)(2,1)}), bf16[4,256,1024]{2,1,0:T(8,128)(2,1)}) %all-gather.30.cloned.1.call-update) | async-done | bytes 2097168 | tf_op jit(solution)/shard_map/all_gather | solution.py:86
  631.1 11.2 fusion.28
  645.1 10.2 fusion.32
  655.3 54.4 %reduce-scatter.16.cloned.1.call-done = f32[2,256,1024]{2,1,0:T(8,128)} async-done(((f32[4,256,1024]{2,1,0:T(8,128)}), f32[2,256,1024]{2,1,0:T(8,128)}) %reduce-scatter.16.cloned.1.call-update) | async-done | bytes 2097168 | tf_op jit(solution)/shard_map/reduce_scatter | solution.py:90
  717.0 33.0 %all-gather.32.cloned.1.call-done = bf16[4,256,1024]{2,1,0:T(8,128)(2,1)} async-done(((bf16[2,256,1024]{2,1,0:T(8,128)(2,1)}), bf16[4,256,1024]{2,1,0:T(8,128)(2,1)}) %all-gather.32.cloned.1.call-update) | async-done | bytes 2097168 | tf_op jit(solution)/shard_map/all_gather | solution.py:86
  772.4 7.6 fusion.35
  781.9 7.1 convolution_bitcast_fusion.1
  794.5 12.8 convolution_bitcast_fusion
  809.1 7.1 convolution_bitcast_fusion.2
  816.3 18.1 %reduce-scatter.26.cloned.1.call-done = f32[2,256,1024]{2,1,0:T(8,128)} async-done(((f32[4,256,1024]{2,1,0:T(8,128)}), f32[2,256,1024]{2,1,0:T(8,128)}) %reduce-scatter.26.cloned.1.call-update) | async-done | bytes 2097168 | tf_op jit(solution)/shard_map/reduce_scatter | solution.py:90
  836.7 6.1 fusion.12
  872.1 51.5 %reduce-scatter.24.cloned.1.call-done = f32[1536,64]{0,1:T(8,128)} async-done(((f32[1536,1024]{0,1:T(8,128)}), f32[1536,64]{0,1:T(8,128)}) %reduce-scatter.24.cloned.1.call-update) | async-done | bytes 393232 | tf_op jit(solution)/shard_map/reduce_scatter | solution.py:299
  925.3 63.1 %reduce-scatter.20.cloned.1.call-done = f32[512,64]{0,1:T(8,128)} async-done(((f32[512,1024]{0,1:T(8,128)}), f32[512,64]{0,1:T(8,128)}) %reduce-scatter.20.cloned.1.call-update) | async-done | bytes 131088 | tf_op jit(solution)/shard_map/reduce_scatter | solution.py:297
  989.9 136.0 %reduce-scatter.22.cloned.1.call-done = f32[64,2,1536]{2,0,1:T(8,128)} async-done(((f32[1024,2,1536]{2,0,1:T(8,128)}), f32[64,2,1536]{2,0,1:T(8,128)}) %reduce-scatter.22.cloned.1.call-update) | async-done | bytes 786448 | tf_op jit(solution)/shard_map/reduce_scatter | solution.py:298
  1127.9 86.4 %reduce-scatter.18.cloned.1.call-done = f32[64,3,512]{2,0,1:T(8,128)} async-done(((f32[1024,3,512]{2,0,1:T(8,128)}), f32[64,3,512]{2,0,1:T(8,128)}) %reduce-scatter.18.cloned.1.call-update) | async-done | bytes 393232 | tf_op jit(solution)/shard_map/reduce_scatter | solution.py:296
  1218.6 102.8 %reduce-scatter.30.cloned.1.call-done = f32[1001,24]{0,1:T(8,128)} async-done(((f32[1001,768]{0,1:T(8,128)}), f32[1001,24]{0,1:T(8,128)}) %reduce-scatter.30.cloned.1.call-update) | async-done | bytes 96112 | tf_op jit(solution)/shard_map/reduce_scatter | solution.py:312
  1322.9 118.4 %reduce-scatter.28.cloned.1.call-done = f32[2,24,1024]{2,1,0:T(8,128)} async-done(((f32[2,768,1024]{2,1,0:T(8,128)}), f32[2,24,1024]{2,1,0:T(8,128)}) %reduce-scatter.28.cloned.1.call-update) | async-done | bytes 196624 | tf_op jit(solution)/shard_map/reduce_scatter | solution.py:311
  1444.1 158.1 %reduce-scatter.32.cloned.1.call-done = f32[24,4096]{1,0:T(8,128)} async-done(((f32[768,4096]{1,0:T(8,128)}), f32[24,4096]{1,0:T(8,128)}) %reduce-scatter.32.cloned.1.call-update) | async-done | bytes 393232 | tf_op jit(solution)/shard_map/reduce_scatter | solution.py:313
  1604.6 40.2 %all-reduce = (f32[]{:T(128)}, f32[]{:T(128)}) all-reduce(f32[]{:T(128)} %multiply_reduce_fusion.21, f32[]{:T(128)S(6)} %add.296), channel_id=1, replica_groups=mesh['dp'=16,'tensor'=2] {'dp','tensor'}, use_global_device_ids=true, to_apply=%region_11.12 | all-reduce | flops 2 | bytes 16 | tf_op jit(solution)/shard_map/psum | solution.py:281
  (327 shorter events, 165.2 us)
Async XLA Ops:
  7.2 66.2 %all-gather.12.cloned.1.call-start = ((), (), s32[]{:S(2)}) async-start(), calls=%async_computation.11 | async-start | bytes 3244032 | tf_op jit(solution)/shard_map/all_gather | solution.py:260
  8.8 136.3 %all-gather.16.cloned.1.call-start = ((), (), s32[]{:S(2)}) async-start(), calls=%async_computation.13 | async-start | bytes 6488064 | tf_op jit(solution)/shard_map/all_gather | solution.py:262
  10.6 191.6 %all-gather.14.cloned.1.call-start = ((), (), s32[]{:S(2)}) async-start(), calls=%async_computation.12 | async-start | bytes 1622016 | tf_op jit(solution)/shard_map/all_gather | solution.py:261
  12.2 236.7 %all-gather.20.cloned.1.call-start = ((), (), s32[]{:S(2)}) async-start(), calls=%async_computation.15 | async-start | bytes 3342336 | tf_op jit(solution)/shard_map/all_gather | solution.py:254
  14.0 268.3 %all-gather.18.cloned.1.call-start = ((), (), s32[]{:S(2)}) async-start(), calls=%async_computation.14 | async-start | bytes 3145728 | tf_op jit(solution)/shard_map/all_gather | solution.py:86
  14.7 187.5 %copy-start.76 = (s32[2]{0:T(128)}, s32[2]{0:T(128)S(1)}, u32[]{:S(2)}) copy-start(s32[2]{0:T(128)S(1)} %compare_select_fusion) | copy-start | bytes 28
  15.9 60.5 %copy-start.82 = (f32[2]{0:T(128)}, f32[2]{0:T(128)S(1)}, u32[]{:S(2)}) copy-start(f32[2]{0:T(128)S(1)} %get-tuple-element.165) | copy-start | bytes 28
  16.0 129.1 %copy-start.72 = (bf16[2,128]{1,0:T(2,128)(2,1)}, bf16[2,128]{1,0:T(2,128)(2,1)S(1)}, u32[]{:S(2)}) copy-start(bf16[2,128]{1,0:T(2,128)(2,1)S(1)} %get-tuple-element.162) | copy-start | bytes 1540
  16.0 129.1 %copy-start.74 = (bf16[2,128]{1,0:T(2,128)(2,1)}, bf16[2,128]{1,0:T(2,128)(2,1)S(1)}, u32[]{:S(2)}) copy-start(bf16[2,128]{1,0:T(2,128)(2,1)S(1)} %get-tuple-element.163) | copy-start | bytes 1540
  76.4 68.7 %copy-start.68 = (f32[2,256]{1,0:T(2,128)}, f32[2,256]{1,0:T(2,128)S(1)}, u32[]{:S(2)}) copy-start(f32[2,256]{1,0:T(2,128)S(1)} %get-tuple-element.168) | copy-start | bytes 6148
  76.4 133.8 %copy-start.4 = (f32[2,256,1024]{2,1,0:T(8,128)}, f32[2,256,1024]{2,1,0:T(8,128)S(1)}, u32[]{:S(2)}) copy-start(f32[2,256,1024]{2,1,0:T(8,128)S(1)} %get-tuple-element.169) | copy-start | bytes 6291460
  76.4 133.8 %copy-start.64 = (f32[2,256]{1,0:T(2,128)}, f32[2,256]{1,0:T(2,128)S(1)}, u32[]{:S(2)}) copy-start(f32[2,256]{1,0:T(2,128)S(1)} %fusion.85) | copy-start | bytes 6148
  211.5 111.4 %all-gather.22.cloned.1.call-start = ((), (), s32[]{:S(2)}) async-start(), calls=%async_computation.16 | async-start | bytes 1114112 | tf_op jit(solution)/shard_map/all_gather | solution.py:255
  212.2 168.6 %reduce-scatter.12.cloned.1.call-start = ((), (), s32[]{:S(2)}) async-start(), calls=%async_computation.17 | async-start | bytes 6291456 | tf_op jit(solution)/shard_map/reduce_scatter | solution.py:90
  327.4 118.5 %all-gather.26.cloned.1.call-start = ((), (), s32[]{:S(2)}) async-start(), calls=%async_computation.19 | async-start | bytes 6684672 | tf_op jit(solution)/shard_map/all_gather | solution.py:256
  329.4 149.8 %all-gather.24.cloned.1.call-start = ((), (), s32[]{:S(2)}) async-start(), calls=%async_computation.18 | async-start | bytes 3145728 | tf_op jit(solution)/shard_map/all_gather | solution.py:86
  385.7 141.9 %all-gather.28.cloned.1.call-start = ((), (), s32[]{:S(2)}) async-start(), calls=%async_computation.20 | async-start | bytes 3342336 | tf_op jit(solution)/shard_map/all_gather | solution.py:257
  386.5 202.8 %reduce-scatter.14.cloned.1.call-start = ((), (), s32[]{:S(2)}) async-start(), calls=%async_computation.21 | async-start | bytes 6291456 | tf_op jit(solution)/shard_map/reduce_scatter | solution.py:90
  536.0 95.1 %all-gather.30.cloned.1.call-start = ((), (), s32[]{:S(2)}) async-start(), calls=%async_computation.22 | async-start | bytes 3145728 | tf_op jit(solution)/shard_map/all_gather | solution.py:86
  597.8 111.9 %reduce-scatter.16.cloned.1.call-start = ((), (), s32[]{:S(2)}) async-start(), calls=%async_computation.23 | async-start | bytes 6291456 | tf_op jit(solution)/shard_map/reduce_scatter | solution.py:90
  655.3 94.8 %all-gather.32.cloned.1.call-start = ((), (), s32[]{:S(2)}) async-start(), calls=%async_computation.24 | async-start | bytes 3145728 | tf_op jit(solution)/shard_map/all_gather | solution.py:86
  716.8 117.6 %reduce-scatter.26.cloned.1.call-start = ((), (), s32[]{:S(2)}) async-start(), calls=%async_computation.29 | async-start | bytes 6291456 | tf_op jit(solution)/shard_map/reduce_scatter | solution.py:90
  780.0 143.6 %reduce-scatter.24.cloned.1.call-start = ((), (), s32[]{:S(2)}) async-start(), calls=%async_computation.28 | async-start | bytes 6684672 | tf_op jit(solution)/shard_map/reduce_scatter | solution.py:299
  789.0 199.4 %reduce-scatter.20.cloned.1.call-start = ((), (), s32[]{:S(2)}) async-start(), calls=%async_computation.26 | async-start | bytes 2228224 | tf_op jit(solution)/shard_map/reduce_scatter | solution.py:297
  794.5 331.5 %reduce-scatter.22.cloned.1.call-start = ((), (), s32[]{:S(2)}) async-start(), calls=%async_computation.27 | async-start | bytes 13369344 | tf_op jit(solution)/shard_map/reduce_scatter | solution.py:298
  807.3 407.0 %reduce-scatter.18.cloned.1.call-start = ((), (), s32[]{:S(2)}) async-start(), calls=%async_computation.25 | async-start | bytes 6684672 | tf_op jit(solution)/shard_map/reduce_scatter | solution.py:296
  816.3 505.1 %reduce-scatter.30.cloned.1.call-start = ((), (), s32[]{:S(2)}) async-start(), calls=%async_computation.31 | async-start | bytes 3244032 | tf_op jit(solution)/shard_map/reduce_scatter | solution.py:312
  848.7 592.5 %reduce-scatter.28.cloned.1.call-start = ((), (), s32[]{:S(2)}) async-start(), calls=%async_computation.30 | async-start | bytes 6488064 | tf_op jit(solution)/shard_map/reduce_scatter | solution.py:311
  859.2 743.1 %reduce-scatter.32.cloned.1.call-start = ((), (), s32[]{:S(2)}) async-start(), calls=%async_computation.32 | async-start | bytes 12976128 | tf_op jit(solution)/shard_map/reduce_scatter | solution.py:313
  870.6 774.9 %copy-start.17 = (f32[64,2,1536]{2,1,0:T(2,128)S(1)}, f32[64,2,1536]{2,1,0:T(2,128)}, u32[]{:S(2)}) copy-start(f32[64,2,1536]{2,1,0:T(2,128)} %param.41) | copy-start | bytes 2359300
  870.6 774.9 %copy-start.38 = (f32[64,2,1536]{2,1,0:T(2,128)S(1)}, f32[64,2,1536]{2,1,0:T(2,128)}, u32[]{:S(2)}) copy-start(f32[64,2,1536]{2,1,0:T(2,128)} %param.43) | copy-start | bytes 2359300
  870.6 775.0 %copy-start.39 = (f32[64,2,1536]{2,1,0:T(2,128)S(1)}, f32[64,2,1536]{2,1,0:T(2,128)}, u32[]{:S(2)}) copy-start(f32[64,2,1536]{2,1,0:T(2,128)} %param.42) | copy-start | bytes 2359300
  (85 other events, 632.4 us)
Sparse Core Ops, SparseCore 0:
  11.5 61.7 all-gather.11
  76.8 68.2 all-gather.15
  148.6 53.5 all-gather.13
  204.8 44.0 all-gather.19
  250.3 31.9 all-gather.17
  284.9 37.9 all-gather.21
  327.5 53.2 reduce-scatter.11
  383.9 61.9 all-gather.25
  447.5 31.6 all-gather.23
  482.2 45.4 all-gather.27
  536.2 53.0 reduce-scatter.13
  597.9 33.1 all-gather.29
  655.4 54.2 reduce-scatter.15
  716.9 33.1 all-gather.31
  780.1 54.2 reduce-scatter.25
  838.2 85.3 reduce-scatter.23
  927.7 60.6 reduce-scatter.19
  992.3 133.5 reduce-scatter.21
  1129.9 84.3 reduce-scatter.17
  1220.4 100.8 reduce-scatter.29
  1327.9 113.2 reduce-scatter.27
  1447.3 154.9 reduce-scatter.31
where the time goes:
time: 1680 us; the launch traced here: 1670 us
  waiting for transfers between devices  1360 us (81%)
  matrix products  143 us (9%)
  other arithmetic  62.7 us (4%)
  blocking collectives  40.2 us (2%)
  local copies, waits for them, and re-layouts  36.4 us (2%)
  between operations  23 us (1%)
    reduce_scatter x4, waiting for transfers between devices, pair_sum(): return lax.psum_scatter(value, 'tensor', scatter_dimension=0, tiled=True)  176 us
    reduce_scatter x1, waiting for transfers between devices, body(): lax.psum_scatter(mapping_grad, ('dp', 'tensor'), scatter_dimension=0, til...  158 us
    reduce_scatter x1, waiting for transfers between devices, body(): lax.psum_scatter(big_grads[2], 'dp', scatter_dimension=0, tiled=True)  136 us
    all_gather x4, waiting for transfers between devices, pair_rows(): return lax.all_gather(value, 'tensor', axis=0, tiled=True)  133 us
    reduce_scatter x1, waiting for transfers between devices, body(): lax.psum_scatter(patch_grads, ('dp', 'tensor'), scatter_dimension=1, tile...  118 us
    dot_general x23, matrix products, einsum_low(): return jnp.einsum(form, left, right, preferred_element_type=jnp.float32)  118 us
    reduce_scatter x1, waiting for transfers between devices, body(): lax.psum_scatter(table_grad, ('dp', 'tensor'), scatter_dimension=1, tiled...  103 us
    reduce_scatter x1, waiting for transfers between devices, body(): lax.psum_scatter(big_grads[0], 'dp', scatter_dimension=0, tiled=True)  86.4 us
  transfers between devices with their start and end apart: 22, of which 22 were waited for; matrix products, arithmetic and copies ran while one was open for 8% of the time, Pallas kernels for 0%

commit v1 on v0

--- a/solution.py
+++ b/solution.py
@@ -1,3 +1,4 @@
+import functools
 import math
 import jax
 import jax.numpy as jnp
@@ -22,6 +23,38 @@
 ADAM_EPS = 1e-08
 CLIP = 0.02
 NORM_EPS = 1e-06
+
+
+def manage_state(obj, lane_axis, dimension_no):
+    piece_out, seen_now, latest = (
+        jax.lax.axis_size(lane_axis),
+        jax.lax.axis_index(lane_axis),
+        obj.shape[dimension_no],
+    )
+    pool = list(map(lambda tick: (tick, (tick + 1) % piece_out), range(piece_out)))
+    series = list(map(lambda tick: (tick, (tick - 1) % piece_out), range(piece_out)))
+    outer = jnp.zeros(
+        (*obj.shape[:dimension_no], piece_out * latest, *obj.shape[dimension_no + 1 :]), obj.dtype
+    )
+    y = taken_in = obj
+    outer = lax.dynamic_update_slice_in_dim(outer, obj, seen_now * latest, axis=dimension_no)
+    m = 1
+    next_value = piece_out // 2
+    while m < next_value + 1:
+        y = jax.lax.ppermute(y, lane_axis, pool)
+        outer = lax.dynamic_update_slice_in_dim(
+            outer, y, (seen_now - m) % piece_out * latest, axis=dimension_no
+        )
+        if m < piece_out - next_value:
+            taken_in = jax.lax.ppermute(taken_in, lane_axis, series)
+            outer = lax.dynamic_update_slice_in_dim(
+                outer, taken_in, (seen_now + m) % piece_out * latest, axis=dimension_no
+            )
+        m = m + 1
+    return outer
+
+
+extend_floor = functools.partial(manage_state, lane_axis="dp", dimension_no=0)
 
 
 def to_low(value):
@@ -251,7 +284,7 @@
         second_mapping,
     )
     big = (
-        lax.all_gather(inward.astype(jnp.bfloat16), "dp", axis=0, tiled=True),
+        extend_floor(inward.astype(jnp.bfloat16)),
         lax.all_gather(outward.astype(jnp.bfloat16), "dp", axis=1, tiled=True),
         lax.all_gather(expand.astype(jnp.bfloat16), "dp", axis=0, tiled=True),
         lax.all_gather(shrink.astype(jnp.bfloat16), "dp", axis=1, tiled=True),

time: 1680 us -> 1670 us (level)
  waiting for transfers between devices: 1360 us -> 1320 us
  starting transfers between devices: 2.17 us -> 34.3 us
    all_gather x4, waiting for transfers between devices: 133 us -> 98.5 us  [pair_rows(): return lax.all_gather(value, 'tensor', axis=0, tiled=True)]
    ppermute x0 -> x15, starting transfers between devices: none -> 31.7 us  [the longest x7 31.1 us: manage_state(): taken_in = jax.lax.ppermute(taken_in, lane_axis, series)]
    ppermute x0 -> x15, waiting for transfers between devices: none -> 30.7 us  [the longest x8 30.7 us: manage_state(): y = jax.lax.ppermute(y, lane_axis, pool)]
    all_gather x1, waiting for transfers between devices: 24.3 us -> 0.02 us  [body(): lax.all_gather(outward.astype(jnp.bfloat16), 'dp', axis=1, tiled=True)]
  transfers between devices with their start and end apart: 22 -> 37, of which waited for: 22 -> 28; matrix products, arithmetic and copies ran while one was open for 8% -> 9% of each run, Pallas kernels for 0% -> 0%
where the time goes in v1:
time: 1670 us; the launch traced here: 1660 us
  waiting for transfers between devices  1320 us (79%)
  matrix products  145 us (9%)
  other arithmetic  65.2 us (4%)
  blocking collectives  40.2 us (2%)
  local copies, waits for them, and re-layouts  35.4 us (2%)
  starting transfers between devices  34.3 us (2%)
  between operations  23.3 us (1%)
    reduce_scatter x4, waiting for transfers between devices, pair_sum(): return lax.psum_scatter(value, 'tensor', scatter_dimension=0, tiled=True)  174 us
    reduce_scatter x1, waiting for transfers between devices, body(): lax.psum_scatter(mapping_grad, ('dp', 'tensor'), scatter_dimension=0, til...  158 us
    reduce_scatter x1, waiting for transfers between devices, body(): lax.psum_scatter(big_grads[2], 'dp', scatter_dimension=0, tiled=True)  136 us
    dot_general x23, matrix products, einsum_low(): return jnp.einsum(form, left, right, preferred_element_type=jnp.float32)  119 us
    reduce_scatter x1, waiting for transfers between devices, body(): lax.psum_scatter(patch_grads, ('dp', 'tensor'), scatter_dimension=1, tile...  118 us
    reduce_scatter x1, waiting for transfers between devices, body(): lax.psum_scatter(table_grad, ('dp', 'tensor'), scatter_dimension=1, tiled...  103 us
    all_gather x4, waiting for transfers between devices, pair_rows(): return lax.all_gather(value, 'tensor', axis=0, tiled=True)  98.5 us
    reduce_scatter x1, waiting for transfers between devices, body(): lax.psum_scatter(big_grads[0], 'dp', scatter_dimension=0, tiled=True)  86.4 us
  transfers between devices with their start and end apart: 37, of which 28 were waited for; matrix products, arithmetic and copies ran while one was open for 9% of the time, Pallas kernels for 0%

profile of v1, /device:TPU:0, one launch (start us, length us, event | category | flops | bytes accessed | tf_op | source)
XLA Modules:
  0.0 1659.6 jit_solution(10706130411443486422)
XLA Ops:
  14.3 59.1 %all-gather.12.cloned.1.call-done = bf16[2,768,1024]{2,1,0:T(8,128)(2,1)} async-done(((bf16[2,24,1024]{2,1,0:T(8,128)(2,1)}), bf16[2,768,1024]{2,1,0:T(8,128)(2,1)}) %all-gather.12.cloned.1.call-update) | async-done | bytes 3145744 | tf_op jit(solution)/shard_map/all_gather | solution.py:293
  76.4 68.7 %all-gather.16.cloned.1.call-done = bf16[768,4096]{1,0:T(8,128)(2,1)} async-done(((bf16[24,4096]{1,0:T(8,128)(2,1)}), bf16[768,4096]{1,0:T(8,128)(2,1)}) %all-gather.16.cloned.1.call-update) | async-done | bytes 6291472 | tf_op jit(solution)/shard_map/all_gather | solution.py:295
  146.3 55.9 %all-gather.14.cloned.1.call-done = bf16[1001,768]{0,1:T(8,128)(2,1)} async-done(((bf16[1001,24]{0,1:T(8,128)(2,1)}), bf16[1001,768]{0,1:T(8,128)(2,1)}) %all-gather.14.cloned.1.call-update) | async-done | bytes 1537552 | tf_op jit(solution)/shard_map/all_gather | solution.py:294
  269.0 8.2 collective-permute-done.14
  277.2 5.2 fusion.29
  299.9 49.5 %reduce-scatter.12.cloned.1.call-done = f32[2,256,1024]{2,1,0:T(8,128)} async-done(((f32[4,256,1024]{2,1,0:T(8,128)}), f32[2,256,1024]{2,1,0:T(8,128)}) %reduce-scatter.12.cloned.1.call-update) | async-done | bytes 2097168 | tf_op jit(solution)/shard_map/reduce_scatter | solution.py:123
  354.4 60.1 %all-gather.24.cloned.1.call-done = bf16[1024,2,1536]{2,0,1:T(8,128)(2,1)} async-done(((bf16[64,2,1536]{2,0,1:T(8,128)(2,1)}), bf16[1024,2,1536]{2,0,1:T(8,128)(2,1)}) %all-gather.24.cloned.1.call-update) | async-done | bytes 6291472 | tf_op jit(solution)/shard_map/all_gather | solution.py:289
  414.5 33.4 %all-gather.22.cloned.1.call-done = bf16[4,256,1024]{2,1,0:T(8,128)(2,1)} async-done(((bf16[2,256,1024]{2,1,0:T(8,128)(2,1)}), bf16[4,256,1024]{2,1,0:T(8,128)(2,1)}) %all-gather.22.cloned.1.call-update) | async-done | bytes 2097168 | tf_op jit(solution)/shard_map/all_gather | solution.py:119
  447.9 9.4 fusion.9
  465.3 30.9 %all-gather.26.cloned.1.call-done = bf16[1536,1024]{0,1:T(8,128)(2,1)} async-done(((bf16[1536,64]{0,1:T(8,128)(2,1)}), bf16[1536,1024]{0,1:T(8,128)(2,1)}) %all-gather.26.cloned.1.call-update) | async-done | bytes 3145744 | tf_op jit(solution)/shard_map/all_gather | solution.py:290
  496.2 8.3 fusion.24
  505.4 52.4 %reduce-scatter.14.cloned.1.call-done = f32[2,256,1024]{2,1,0:T(8,128)} async-done(((f32[4,256,1024]{2,1,0:T(8,128)}), f32[2,256,1024]{2,1,0:T(8,128)}) %reduce-scatter.14.cloned.1.call-update) | async-done | bytes 2097168 | tf_op jit(solution)/shard_map/reduce_scatter | solution.py:123
  566.9 32.6 %all-gather.28.cloned.1.call-done = bf16[4,256,1024]{2,1,0:T(8,128)(2,1)} async-done(((bf16[2,256,1024]{2,1,0:T(8,128)(2,1)}), bf16[4,256,1024]{2,1,0:T(8,128)(2,1)}) %all-gather.28.cloned.1.call-update) | async-done | bytes 2097168 | tf_op jit(solution)/shard_map/all_gather | solution.py:119
  599.5 11.3 fusion.28
  613.4 10.1 fusion.32
  623.6 54.4 %reduce-scatter.16.cloned.1.call-done = f32[2,256,1024]{2,1,0:T(8,128)} async-done(((f32[4,256,1024]{2,1,0:T(8,128)}), f32[2,256,1024]{2,1,0:T(8,128)}) %reduce-scatter.16.cloned.1.call-update) | async-done | bytes 2097168 | tf_op jit(solution)/shard_map/reduce_scatter | solution.py:123
  685.9 32.5 %all-gather.30.cloned.1.call-done = bf16[4,256,1024]{2,1,0:T(8,128)(2,1)} async-done(((bf16[2,256,1024]{2,1,0:T(8,128)(2,1)}), bf16[4,256,1024]{2,1,0:T(8,128)(2,1)}) %all-gather.30.cloned.1.call-update) | async-done | bytes 2097168 | tf_op jit(solution)/shard_map/all_gather | solution.py:119
  744.7 22.0 %all-gather.32.cloned.1.call-done = bf16[1024,3,512]{2,0,1:T(8,128)(2,1)} async-done(((bf16[64,3,512]{2,0,1:T(8,128)(2,1)}), bf16[1024,3,512]{2,0,1:T(8,128)(2,1)}) %all-gather.32.cloned.1.call-update) | async-done | bytes 3145744 | tf_op jit(solution)/shard_map/all_gather | solution.py:317
  766.7 7.6 fusion.35
  776.2 7.0 convolution_bitcast_fusion.1
  788.8 12.6 convolution_bitcast_fusion
  803.2 7.1 convolution_bitcast_fusion.2
  810.4 17.2 %reduce-scatter.26.cloned.1.call-done = f32[2,256,1024]{2,1,0:T(8,128)} async-done(((f32[4,256,1024]{2,1,0:T(8,128)}), f32[2,256,1024]{2,1,0:T(8,128)}) %reduce-scatter.26.cloned.1.call-update) | async-done | bytes 2097168 | tf_op jit(solution)/shard_map/reduce_scatter | solution.py:123
  829.8 6.1 fusion.12
  865.3 51.4 %reduce-scatter.24.cloned.1.call-done = f32[1536,64]{0,1:T(8,128)} async-done(((f32[1536,1024]{0,1:T(8,128)}), f32[1536,64]{0,1:T(8,128)}) %reduce-scatter.24.cloned.1.call-update) | async-done | bytes 393232 | tf_op jit(solution)/shard_map/reduce_scatter | solution.py:332
  918.4 63.2 %reduce-scatter.20.cloned.1.call-done = f32[512,64]{0,1:T(8,128)} async-done(((f32[512,1024]{0,1:T(8,128)}), f32[512,64]{0,1:T(8,128)}) %reduce-scatter.20.cloned.1.call-update) | async-done | bytes 131088 | tf_op jit(solution)/shard_map/reduce_scatter | solution.py:330
  983.2 136.1 %reduce-scatter.22.cloned.1.call-done = f32[64,2,1536]{2,0,1:T(8,128)} async-done(((f32[1024,2,1536]{2,0,1:T(8,128)}), f32[64,2,1536]{2,0,1:T(8,128)}) %reduce-scatter.22.cloned.1.call-update) | async-done | bytes 786448 | tf_op jit(solution)/shard_map/reduce_scatter | solution.py:331
  1121.2 86.4 %reduce-scatter.18.cloned.1.call-done = f32[64,3,512]{2,0,1:T(8,128)} async-done(((f32[1024,3,512]{2,0,1:T(8,128)}), f32[64,3,512]{2,0,1:T(8,128)}) %reduce-scatter.18.cloned.1.call-update) | async-done | bytes 393232 | tf_op jit(solution)/shard_map/reduce_scatter | solution.py:329
  1211.9 102.7 %reduce-scatter.30.cloned.1.call-done = f32[1001,24]{0,1:T(8,128)} async-done(((f32[1001,768]{0,1:T(8,128)}), f32[1001,24]{0,1:T(8,128)}) %reduce-scatter.30.cloned.1.call-update) | async-done | bytes 96112 | tf_op jit(solution)/shard_map/reduce_scatter | solution.py:345
  1316.1 118.3 %reduce-scatter.28.cloned.1.call-done = f32[2,24,1024]{2,1,0:T(8,128)} async-done(((f32[2,768,1024]{2,1,0:T(8,128)}), f32[2,24,1024]{2,1,0:T(8,128)}) %reduce-scatter.28.cloned.1.call-update) | async-done | bytes 196624 | tf_op jit(solution)/shard_map/reduce_scatter | solution.py:344
  1437.3 158.1 %reduce-scatter.32.cloned.1.call-done = f32[24,4096]{1,0:T(8,128)} async-done(((f32[768,4096]{1,0:T(8,128)}), f32[24,4096]{1,0:T(8,128)}) %reduce-scatter.32.cloned.1.call-update) | async-done | bytes 393232 | tf_op jit(solution)/shard_map/reduce_scatter | solution.py:346
  1597.7 40.2 %all-reduce = (f32[]{:T(128)}, f32[]{:T(128)}) all-reduce(f32[]{:T(128)} %multiply_reduce_fusion.21, f32[]{:T(128)S(6)} %add.457), channel_id=1, replica_groups=mesh['dp'=16,'tensor'=2] {'dp','tensor'}, use_global_device_ids=true, to_apply=%region_11.12 | all-reduce | flops 2 | bytes 16 | tf_op jit(solution)/shard_map/psum | solution.py:314
  (366 shorter events, 218.3 us)
Async XLA Ops:
  7.2 66.2 %all-gather.12.cloned.1.call-start = ((), (), s32[]{:S(2)}) async-start(), calls=%async_computation.11 | async-start | bytes 3244032 | tf_op jit(solution)/shard_map/all_gather | solution.py:293
  8.8 136.3 %all-gather.16.cloned.1.call-start = ((), (), s32[]{:S(2)}) async-start(), calls=%async_computation.13 | async-start | bytes 6488064 | tf_op jit(solution)/shard_map/all_gather | solution.py:295
  10.6 191.6 %all-gather.14.cloned.1.call-start = ((), (), s32[]{:S(2)}) async-start(), calls=%async_computation.12 | async-start | bytes 1622016 | tf_op jit(solution)/shard_map/all_gather | solution.py:294
  12.2 265.0 %all-gather.18.cloned.1.call-start = ((), (), s32[]{:S(2)}) async-start(), calls=%async_computation.14 | async-start | bytes 3145728 | tf_op jit(solution)/shard_map/all_gather | solution.py:119
  211.5 81.5 %all-gather.20.cloned.1.call-start = ((), (), s32[]{:S(2)}) async-start(), calls=%async_computation.15 | async-start | bytes 1114112 | tf_op jit(solution)/shard_map/all_gather | solution.py:288
  212.5 8.1 collective-permute-start
  218.5 130.9 %reduce-scatter.12.cloned.1.call-start = ((), (), s32[]{:S(2)}) async-start(), calls=%async_computation.16 | async-start | bytes 6291456 | tf_op jit(solution)/shard_map/reduce_scatter | solution.py:123
  220.6 7.9 collective-permute-start.2
  220.6 7.9 collective-permute-start.3
  236.4 7.9 collective-permute-start.6
  236.4 7.9 collective-permute-start.7
  252.1 8.4 collective-permute-start.10
  252.1 8.4 collective-permute-start.11
  260.5 8.1 collective-permute-start.12
  260.5 8.4 collective-permute-start.13
  268.6 8.5 collective-permute-start.14
  297.9 116.6 %all-gather.24.cloned.1.call-start = ((), (), s32[]{:S(2)}) async-start(), calls=%async_computation.18 | async-start | bytes 6684672 | tf_op jit(solution)/shard_map/all_gather | solution.py:289
  299.9 148.0 %all-gather.22.cloned.1.call-start = ((), (), s32[]{:S(2)}) async-start(), calls=%async_computation.17 | async-start | bytes 3145728 | tf_op jit(solution)/shard_map/all_gather | solution.py:119
  353.2 143.0 %all-gather.26.cloned.1.call-start = ((), (), s32[]{:S(2)}) async-start(), calls=%async_computation.19 | async-start | bytes 3342336 | tf_op jit(solution)/shard_map/all_gather | solution.py:290
  354.0 203.8 %reduce-scatter.14.cloned.1.call-start = ((), (), s32[]{:S(2)}) async-start(), calls=%async_computation.20 | async-start | bytes 6291456 | tf_op jit(solution)/shard_map/reduce_scatter | solution.py:123
  504.5 95.0 %all-gather.28.cloned.1.call-start = ((), (), s32[]{:S(2)}) async-start(), calls=%async_computation.21 | async-start | bytes 3145728 | tf_op jit(solution)/shard_map/all_gather | solution.py:119
  566.3 111.8 %reduce-scatter.16.cloned.1.call-start = ((), (), s32[]{:S(2)}) async-start(), calls=%async_computation.22 | async-start | bytes 6291456 | tf_op jit(solution)/shard_map/reduce_scatter | solution.py:123
  623.6 94.8 %all-gather.30.cloned.1.call-start = ((), (), s32[]{:S(2)}) async-start(), calls=%async_computation.23 | async-start | bytes 3145728 | tf_op jit(solution)/shard_map/all_gather | solution.py:119
  685.1 81.6 %all-gather.32.cloned.1.call-start = ((), (), s32[]{:S(2)}) async-start(), calls=%async_computation.28 | async-start | bytes 3342336 | tf_op jit(solution)/shard_map/all_gather | solution.py:317
  685.7 141.9 %reduce-scatter.26.cloned.1.call-start = ((), (), s32[]{:S(2)}) async-start(), calls=%async_computation.29 | async-start | bytes 6291456 | tf_op jit(solution)/shard_map/reduce_scatter | solution.py:123
  774.3 142.3 %reduce-scatter.24.cloned.1.call-start = ((), (), s32[]{:S(2)}) async-start(), calls=%async_computation.27 | async-start | bytes 6684672 | tf_op jit(solution)/shard_map/reduce_scatter | solution.py:332
  783.3 198.3 %reduce-scatter.20.cloned.1.call-start = ((), (), s32[]{:S(2)}) async-start(), calls=%async_computation.25 | async-start | bytes 2228224 | tf_op jit(solution)/shard_map/reduce_scatter | solution.py:330
  788.7 330.5 %reduce-scatter.22.cloned.1.call-start = ((), (), s32[]{:S(2)}) async-start(), calls=%async_computation.26 | async-start | bytes 13369344 | tf_op jit(solution)/shard_map/reduce_scatter | solution.py:331
  801.4 406.2 %reduce-scatter.18.cloned.1.call-start = ((), (), s32[]{:S(2)}) async-start(), calls=%async_computation.24 | async-start | bytes 6684672 | tf_op jit(solution)/shard_map/reduce_scatter | solution.py:329
  810.3 504.3 %reduce-scatter.30.cloned.1.call-start = ((), (), s32[]{:S(2)}) async-start(), calls=%async_computation.31 | async-start | bytes 3244032 | tf_op jit(solution)/shard_map/reduce_scatter | solution.py:345
  841.9 592.5 %reduce-scatter.28.cloned.1.call-start = ((), (), s32[]{:S(2)}) async-start(), calls=%async_computation.30 | async-start | bytes 6488064 | tf_op jit(solution)/shard_map/reduce_scatter | solution.py:344
  852.3 743.0 %reduce-scatter.32.cloned.1.call-start = ((), (), s32[]{:S(2)}) async-start(), calls=%async_computation.32 | async-start | bytes 12976128 | tf_op jit(solution)/shard_map/reduce_scatter | solution.py:346
  (97 other events, 3761.6 us)
Sparse Core Ops, SparseCore 0:
  11.5 61.7 all-gather.11
  76.8 68.2 all-gather.15
  148.6 53.5 all-gather.13
  211.6 31.9 all-gather.17
  246.2 40.3 all-gather.19
  298.0 51.3 reduce-scatter.11
  352.5 61.9 all-gather.23
  416.1 31.6 all-gather.21
  451.0 45.1 all-gather.25
  504.6 53.0 reduce-scatter.13
  566.4 33.1 all-gather.27
  623.7 54.2 reduce-scatter.15
  685.2 33.1 all-gather.29
  721.2 45.4 all-gather.31
  774.5 53.0 reduce-scatter.25
  831.4 85.2 reduce-scatter.23
  920.7 60.8 reduce-scatter.19
  985.5 133.6 reduce-scatter.21
  1123.2 84.3 reduce-scatter.17
  1213.7 100.8 reduce-scatter.29
  1321.2 113.1 reduce-scatter.27
  1440.4 154.9 reduce-scatter.31
